TPU v7x, 256 devices: a whole 4x4x8 slice. The times are simulated.
256 devices in a mesh: section: 8 (over y, x_lo), dev: 32 (over x_hi, z, core).
Axes of the slice: x: 4 (x_hi: 2, x_lo: 2; x = x_hi * 2 + x_lo), y: 4, z: 8, core: 2. Of those that a mesh axis runs over, the one named last changes fastest.
Arguments:
- acts: bfloat16 [2, 2048, 12288], P(None, None, ('section', 'dev')), may hold values from -45 to 45
- ln_gain: float32 [12288], P('section'), may hold values from 0.25 to 1.75
- ln_bias: float32 [12288], P('section'), may hold values from -3 to 3
- up_weight: bfloat16 [12288, 24576], P('section', 'dev'), may hold values from -0.0546875 to 0.0546875
- up_bias: float32 [24576], P('dev'), may hold values from -3 to 3
- down_weight: bfloat16 [24576, 6144], P('dev', 'section'), may hold values from -0.0390625 to 0.0390625
- down_bias: float32 [6144], P('section'), may hold values from -3 to 3
Outputs:
- layer_out: bfloat16 [2, 2048, 6144], P(None, 'dev', 'section')
All inputs are finite; a program needn't handle non-finite values.
Results may differ from a plain program's by a relative error of at most 0.025.
Values may be sent and summed in bfloat16 or wider, within the bound.
No kernel may reach another device: no remote copies, remote signals or barrier semaphores. Data moves between devices by JAX's collectives and lax.ppermute only.
A program may use at most 64 MiB of HBM per device.

v0:
```python
import jax
import jax.numpy as jnp
from jax import lax
from jax.sharding import PartitionSpec as P


def local(acts, ln_gain, ln_bias, up_weight, up_bias, down_weight, down_bias):
    micros, seq_all, slim = acts.shape
    devices = lax.axis_size("dev")
    local_seq = seq_all // devices
    rows_here = micros * local_seq
    feature_total = ln_gain.shape[0] * lax.axis_size("section")
    moved = lax.all_to_all(acts, "dev", split_axis=1, concat_axis=2, tiled=True)
    widened = moved.reshape(rows_here, -1).astype(jnp.float32)
    center = lax.psum(jnp.sum(widened, axis=1), "section") / feature_total
    deviation = widened - center[:, None]
    spread = lax.psum(jnp.sum(deviation * deviation, axis=1), "section") / feature_total
    normed_local = (deviation * lax.rsqrt(spread + 1e-05)[:, None] * ln_gain + ln_bias).astype(
        jnp.bfloat16
    )
    partial_up = jnp.dot(
        lax.all_gather(normed_local, "dev", axis=0, tiled=True),
        up_weight,
        preferred_element_type=jnp.float32,
    )
    shared = lax.psum_scatter(
        partial_up.astype(jnp.bfloat16), "section", scatter_dimension=0, tiled=True
    ).astype(jnp.float32)
    hidden_share = jax.nn.gelu(shared + up_bias, approximate=True).astype(jnp.bfloat16)
    hidden = lax.all_gather(hidden_share, "section", axis=0, tiled=True)
    summed = lax.psum_scatter(
        jnp.dot(hidden, down_weight, preferred_element_type=jnp.float32).astype(jnp.bfloat16),
        "dev",
        scatter_dimension=0,
        tiled=True,
    ).astype(jnp.float32)
    return (summed + down_bias).astype(jnp.bfloat16).reshape(micros, local_seq, -1)


def solution(mesh):
    in_specs = (
        P(None, None, ("section", "dev")),
        P("section"),
        P("section"),
        P("section", "dev"),
        P("dev"),
        P("dev", "section"),
        P("section"),
    )
    out_specs = P(None, "dev", "section")
    return jax.shard_map(local, mesh=mesh, in_specs=in_specs, out_specs=out_specs, check_vma=False)
```

profile of v0, /device:TPU:8, one launch (start us, length us, event | category | flops | bytes accessed | tf_op | source)
XLA Modules:
  0.0 651.6 jit_solution(14507344754320732346)
XLA Ops:
  6.5 2.5 copy.9
  9.0 2.4 reshape.27
  11.4 28.8 %all_to_all.4 = bf16[32,2,3072]{2,1,0:T(2,128)(2,1)} all-to-all(bf16[32,2,3072]{2,1,0:T(2,128)(2,1)} %reshape.27), channel_id=1, replica_groups=mesh['section'=8,'dev'=32] {'dev'}, dimensions={0} | all-to-all | bytes 786432 | tf_op jit(solution)/shard_map/all_to_all | solution.py:13
  40.3 4.8 reshape.28
  45.0 3.6 copy.10
  48.7 3.0 bitcast_reduce_fusion
  51.7 0.1 reduce_sum.23
  51.8 16.8 %psum.14 = f32[128]{0:T(128)S(1)} all-reduce(f32[128]{0:T(128)S(1)} %reduce_sum.23), channel_id=1, replica_groups=mesh['section'=8,'dev'=32] {'section'}, use_global_device_ids=true, to_apply=%region_1.0 | all-reduce | flops 128 | bytes 1024 | tf_op jit(solution)/shard_map/psum | solution.py:15
  68.6 0.1 sub.17
  68.7 3.0 multiply_reduce_fusion
  71.7 0.1 reduce_sum.25
  71.8 16.0 %psum.15 = f32[128]{0:T(128)S(1)} all-reduce(f32[128]{0:T(128)S(1)} %reduce_sum.25), channel_id=1, replica_groups=mesh['section'=8,'dev'=32] {'section'}, use_global_device_ids=true, to_apply=%region_3.0 | all-reduce | flops 128 | bytes 1024 | tf_op jit(solution)/shard_map/psum | solution.py:17
  87.8 2.3 reshape.24
  90.2 1.2 add_convert_fusion
  91.5 0.2 reduce-scatter.3.cloned.1.call-start
  91.7 125.0 %all-gather.3.cloned.1.call-done = bf16[4096,1536]{0,1:T(8,128)(2,1)} async-done(((bf16[128,1536]{0,1:T(8,128)(2,1)}), bf16[4096,1536]{0,1:T(8,128)(2,1)}) %all-gather.3.cloned.1.call-update) | async-done | bytes 12582928 | tf_op jit(solution)/shard_map/all_gather | solution.py:22
  216.7 14.9 %convolution_convert_fusion.1 = bf16[4096,768]{1,0:T(8,128)(2,1)} fusion(bf16[4096,1536]{0,1:T(8,128)(2,1)} %all-gather.3.cloned.1.call-done, bf16[1536,768]{1,0:T(8,128)(2,1)S(1)} %copy-done), kind=kOutput, calls=%fused_computation.1 | convolution fusion | flops 9666822144 | bytes 21233664 | tf_op jit(solution)/shard_map/dot_general | solution.py:21
  231.6 128.6 %reduce-scatter.3.cloned.1.call-done = bf16[512,768]{1,0:T(8,128)(2,1)} async-done(((bf16[4096,768]{1,0:T(8,128)(2,1)}), bf16[512,768]{1,0:T(8,128)(2,1)}) %reduce-scatter.3.cloned.1.call-update) | async-done | bytes 786448 | tf_op jit(solution)/shard_map/reduce_scatter | solution.py:26
  360.3 2.6 fusion.7
  362.9 0.0 reduce-scatter.5.cloned.1.call-start
  363.0 132.7 %all-gather.5.cloned.1.call-done = bf16[4096,768]{1,0:T(8,128)(2,1)} async-done(((bf16[512,768]{1,0:T(8,128)(2,1)}), bf16[4096,768]{1,0:T(8,128)(2,1)}) %all-gather.5.cloned.1.call-update) | async-done | bytes 6291472 | tf_op jit(solution)/shard_map/all_gather | solution.py:30
  495.6 9.7 %convolution_convert_fusion = bf16[4096,768]{1,0:T(8,128)(2,1)} fusion(bf16[4096,768]{1,0:T(8,128)(2,1)} %all-gather.5.cloned.1.call-done, bf16[768,768]{1,0:T(8,128)(2,1)S(1)} %copy-done.5), kind=kOutput, calls=%fused_computation | convolution fusion | flops 4834983936 | bytes 13762560 | tf_op jit(solution)/shard_map/dot_general | solution.py:32
  505.4 138.0 %reduce-scatter.5.cloned.1.call-done = bf16[128,768]{1,0:T(8,128)(2,1)} async-done(((bf16[4096,768]{1,0:T(8,128)(2,1)}), bf16[128,768]{1,0:T(8,128)(2,1)}) %reduce-scatter.5.cloned.1.call-update) | async-done | bytes 196624 | tf_op jit(solution)/shard_map/reduce_scatter | solution.py:31
  643.4 1.6 add_convert_fusion.1
  (20 shorter events, 0.2 us)
Async XLA Ops:
  6.5 210.2 %copy-start = (bf16[1536,768]{1,0:T(8,128)(2,1)S(1)}, bf16[1536,768]{1,0:T(8,128)(2,1)}, u32[]{:S(2)}) copy-start(bf16[1536,768]{1,0:T(8,128)(2,1)} %param.10) | copy-start | bytes 7077892
  6.5 210.1 %all-gather.3.cloned.1.call-start = ((), (), s32[]{:S(2)}) async-start(), calls=%async_computation.3 | async-start | bytes 12976128 | tf_op jit(solution)/shard_map/all_gather | solution.py:22
  71.7 18.5 %copy-start.1 = (f32[1536]{0:T(1024)S(1)}, f32[1536]{0:T(1024)}, u32[]{:S(2)}) copy-start(f32[1536]{0:T(1024)} %param.9) | copy-start | bytes 18436
  71.7 18.5 %copy-start.2 = (f32[1536]{0:T(1024)S(1)}, f32[1536]{0:T(1024)}, u32[]{:S(2)}) copy-start(f32[1536]{0:T(1024)} %param.8) | copy-start | bytes 18436
  91.5 268.8 %reduce-scatter.3.cloned.1.call-start = ((), (), s32[]{:S(2)}) async-start(), calls=%async_computation.4 | async-start | bytes 7077888 | tf_op jit(solution)/shard_map/reduce_scatter | solution.py:26
  231.5 128.7 %copy-start.3 = (f32[768]{0:T(1024)S(1)}, f32[768]{0:T(1024)}, u32[]{:S(2)}) copy-start(f32[768]{0:T(1024)} %param.11) | copy-start | bytes 9220
  231.6 264.1 %copy-start.5 = (bf16[768,768]{1,0:T(8,128)(2,1)S(1)}, bf16[768,768]{1,0:T(8,128)(2,1)}, u32[]{:S(2)}) copy-start(bf16[768,768]{1,0:T(8,128)(2,1)} %param.12) | copy-start | bytes 3538948
  231.6 264.1 %all-gather.5.cloned.1.call-start = ((), (), s32[]{:S(2)}) async-start(), calls=%async_computation.5 | async-start | bytes 7077888 | tf_op jit(solution)/shard_map/all_gather | solution.py:30
  362.9 280.5 %reduce-scatter.5.cloned.1.call-start = ((), (), s32[]{:S(2)}) async-start(), calls=%async_computation.6 | async-start | bytes 6488064 | tf_op jit(solution)/shard_map/reduce_scatter | solution.py:31
  505.4 138.0 %copy-start.4 = (f32[768]{0:T(1024)S(1)}, f32[768]{0:T(1024)}, u32[]{:S(2)}) copy-start(f32[768]{0:T(1024)} %param.13) | copy-start | bytes 9220
Sparse Core Ops, SparseCore 0:
  91.6 125.0 all-gather.2
  231.7 128.5 reduce-scatter.2
  363.0 132.5 all-gather.4
  505.5 137.8 reduce-scatter.4
where the time goes:
time: 652 us
  waiting for transfers between devices  524 us (80%)
  blocking collectives  61.6 us (9%)
  matrix products  24.6 us (4%)
  local copies, waits for them, and re-layouts  15.9 us (2%)
  between operations  13.2 us (2%)
  other arithmetic  11.6 us (2%)
    reduce_scatter x1, waiting for transfers between devices, local(): lax.psum_scatter(jnp.dot(hidden, down_weight, preferred_element_type=jnp....  138 us
    all_gather x1, waiting for transfers between devices, local(): hidden = lax.all_gather(hidden_share, 'section', axis=0, tiled=True)  133 us
    reduce_scatter x1, waiting for transfers between devices, local(): lax.psum_scatter(partial_up.astype(jnp.bfloat16), 'section', scatter_dime...  129 us
    all_gather x1, waiting for transfers between devices, local(): lax.all_gather(normed_local, 'dev', axis=0, tiled=True)  125 us
    all_to_all x1, blocking collectives, local(): moved = lax.all_to_all(acts, 'dev', split_axis=1, concat_axis=2, tiled=True)  28.8 us
    psum x1, blocking collectives, local(): center = lax.psum(jnp.sum(widened, axis=1), 'section') / feature_total  16.8 us
    psum x1, blocking collectives, local(): lax.psum(jnp.sum(deviation * deviation, axis=1), 'section') / feature_total  16 us
    dot_general x1, matrix products, local(): jnp.dot(lax.all_gather(normed_local, 'dev', axis=0, tiled=True), up_weigh...  14.9 us
  transfers between devices with their start and end apart: 4, of which 4 were waited for; matrix products, arithmetic and copies ran while one was open for 0% of the time, Pallas kernels for 0%

commit v1 on v0

v1 whole, which is shorter than its diff:
```python
import jax
import jax.numpy as jnp
from jax import lax
from jax.sharding import Mesh, PartitionSpec as P

f32, bf16 = jnp.float32, jnp.bfloat16
NY, NXLO, NXHI, NZ, NCORE = 4, 2, 2, 8, 2
SEC = ("y", "xlo")
DEV = ("xhi", "z", "core")
NEAR = ("xlo", "xhi", "core")


def swap(x, axis):
    return lax.ppermute(x, axis, [(0, 1), (1, 0)])


def shift(x, d):
    return lax.ppermute(x, "y", [(i, (i + d) % NY) for i in range(NY)])


def near(x, mask):
    return lax.ppermute(x, NEAR, [(i, i ^ mask) for i in range(8)])


def ordered(which, own, other):
    first = which == 0
    return jnp.where(first, own, other), jnp.where(first, other, own)


def local(acts, ln_gain, ln_bias, w1, up_bias, w2, down_bias):
    micros, seq, width = acts.shape
    own_seq = seq // (NXHI * NZ * NCORE)
    chunk = NZ * own_seq
    tokens = NXHI * chunk
    y, xlo, xhi, core = (lax.axis_index(a) for a in ("y", "xlo", "xhi", "core"))
    features = width * 256

    tiles = acts.reshape(micros, NXHI, NZ, NCORE, own_seq, width)
    tiles = tiles.transpose(0, 3, 5, 1, 2, 4).reshape(micros, NCORE, width, tokens)
    mine, theirs = ordered(xlo, tiles[0], tiles[1])
    quarter = [ordered(core, part[0], part[1]) for part in (mine, theirs)]

    def arrived(rx, rh, rc):
        piece, mask = quarter[rx][rc], rx * 4 + rh * 2 + rc
        return near(piece, mask) if mask else piece

    rows = []
    for rx in range(2):
        by_hi = []
        for rh in range(2):
            a, b = ordered(core, arrived(rx, rh, 0), arrived(rx, rh, 1))
            by_hi.append(jnp.concatenate([a, b], axis=0))
        rows.append(jnp.stack(ordered(xhi, *by_hi)))
    x = jnp.stack(rows)

    x, w1 = lax.optimization_barrier((x, w1))
    w1s = [[w1, swap(w1, "core")]]
    far = swap(w1, "xlo")
    w1s.append([far, swap(far, "core")])
    far, w2 = lax.optimization_barrier((far, w2))
    far2 = swap(w2, "xlo")
    w2_cat = jnp.concatenate(
        [
            jnp.concatenate([w2, far2], axis=1),
            jnp.concatenate([swap(w2, "core"), swap(far2, "core")], axis=1),
        ],
        axis=0,
    )
    scale = jnp.stack([ln_gain, ln_bias])
    scale = jnp.stack([scale, swap(scale, "xlo")])
    scale = scale.reshape(NXLO, 2, NXHI, NZ, 2 * width).transpose(1, 3, 0, 2, 4)[..., None]
    biases = [up_bias, swap(up_bias, "core")]

    x32 = x.astype(f32)
    mean = lax.psum(jnp.sum(x32, axis=(0, 1, 2)), ("y", "z")) / features
    off = x32 - mean
    var = lax.psum(jnp.sum(off * off, axis=(0, 1, 2)), ("y", "z")) / features
    rstd = lax.rsqrt(var + 1e-05)

    outs = []
    for t in range(NXHI):
        cut = slice(t * chunk, (t + 1) * chunk)
        gathered = lax.all_gather(x[..., cut], "z")
        normed = (gathered.astype(f32) - mean[cut]) * rstd[cut] * scale[0] + scale[1]
        normed = normed.astype(bf16).transpose(1, 2, 0, 3, 4).reshape(NXLO, -1, chunk)
        part = chunk // NY
        hidden = jnp.zeros((chunk, NCORE * w1.shape[1]), bf16)
        for j in range(NCORE):
            up = sum(
                lax.dot_general(
                    normed[r], w1s[r][j], (((0,), (0,)), ((), ())), preferred_element_type=f32
                )
                for r in range(NXLO)
            ).astype(bf16)
            block = lambda d: lax.dynamic_slice_in_dim(up, (y + d) % NY * part, part, 0)
            total = block(0).astype(f32)
            for d in range(1, NY):
                total = total + shift(block(d), d).astype(f32)
            act = jax.nn.gelu(total + biases[j], approximate=True).astype(bf16)
            for d in range(NY):
                got = shift(act, d) if d else act
                hidden = lax.dynamic_update_slice(
                    hidden, got, ((y - d) % NY * part, j * w1.shape[1])
                )
        down = jnp.dot(hidden, w2_cat, preferred_element_type=f32).astype(bf16)
        outs.append(lax.psum_scatter(down, "z", scatter_dimension=0, tiled=True))

    keep, send = ordered(xhi, outs[0], outs[1])
    cols = down_bias.shape[0]
    here = keep[:, :cols].astype(f32) + near(send[:, :cols], 2).astype(f32)
    other = near(keep[:, cols:], 4).astype(f32) + near(send[:, cols:], 6).astype(f32)
    both = jnp.stack(ordered(xlo, here, other))
    return (both + down_bias).astype(bf16)


def solution(mesh):
    fine = Mesh(mesh.devices.reshape(NY, NXLO, NXHI, NZ, NCORE), SEC + DEV)
    in_specs = (
        P(None, None, SEC + DEV),
        P(SEC),
        P(SEC),
        P(SEC, DEV),
        P(DEV),
        P(DEV, SEC),
        P(SEC),
    )
    return jax.shard_map(
        local, mesh=fine, in_specs=in_specs, out_specs=P(None, DEV, SEC), check_vma=False
    )
```

time: 652 us -> 442 us (0.68); the launches traced: 652 us -> 434 us
  waiting for transfers between devices: 524 us -> 173 us
  blocking collectives: 61.6 us -> 135 us
  starting transfers between devices: 0.31 us -> 64.6 us
    all_gather x2, waiting for transfers between devices: 258 us -> 0.04 us  [local(): gathered = lax.all_gather(x[..., cut], 'z')]
    reduce_scatter x2, waiting for transfers between devices: 267 us -> 65.6 us  [local(): outs.append(lax.psum_scatter(down, 'z', scatter_dimension=0, tiled=True))]
    ppermute x0 -> x42, waiting for transfers between devices: none -> 106 us  [the longest x8 51.2 us: swap(): return lax.ppermute(x, axis, [(0, 1), (1, 0)])]
    psum x2, blocking collectives: 32.8 us -> 135 us  [the longest x1 69.6 us: local(): var = lax.psum(jnp.sum(off * off, axis=(0, 1, 2)), ('y', 'z')) / features]
    ppermute x0 -> x42, starting transfers between devices: none -> 64.5 us  [the longest x24 47.6 us: shift(): return lax.ppermute(x, 'y', [(i, (i + d) % NY) for i in range(NY)])]
    all_to_all x1 -> x0, blocking collectives: 28.8 us -> none  [local(): moved = lax.all_to_all(acts, 'dev', split_axis=1, concat_axis=2, tiled=True)]
    dot_general x2 -> x10, matrix products: 24.6 us -> 29.3 us  [the longest x8 18.4 us: local(): lax.dot_general(normed[r], w1s[r][j], (((0,), (0,)), ((), ())), preferred...]
  transfers between devices with their start and end apart: 4 -> 46, of which waited for: 4 -> 27; matrix products, arithmetic and copies ran while one was open for 0% -> 7% of each run, Pallas kernels for 0% -> 0%
where the time goes in v1:
time: 442 us; the launch traced here: 434 us
  waiting for transfers between devices  173 us (39%)
  blocking collectives  135 us (31%)
  starting transfers between devices  64.6 us (15%)
  matrix products  29.3 us (7%)
  between operations  14 us (3%)
  local copies, waits for them, and re-layouts  9.69 us (2%)
  other arithmetic  7.95 us (2%)
    psum x1, blocking collectives, local(): var = lax.psum(jnp.sum(off * off, axis=(0, 1, 2)), ('y', 'z')) / features  69.6 us
    psum x1, blocking collectives, local(): mean = lax.psum(jnp.sum(x32, axis=(0, 1, 2)), ('y', 'z')) / features  65.8 us
    reduce_scatter x2, waiting for transfers between devices, local(): outs.append(lax.psum_scatter(down, 'z', scatter_dimension=0, tiled=True))  65.6 us
    ppermute x8, waiting for transfers between devices, swap(): return lax.ppermute(x, axis, [(0, 1), (1, 0)])  51.2 us
    ppermute x24, starting transfers between devices, shift(): return lax.ppermute(x, 'y', [(i, (i + d) % NY) for i in range(NY)])  47.6 us
    ppermute x24, waiting for transfers between devices, shift(): return lax.ppermute(x, 'y', [(i, (i + d) % NY) for i in range(NY)])  42.3 us
    dot_general x8, matrix products, local(): lax.dot_general(normed[r], w1s[r][j], (((0,), (0,)), ((), ())), preferred...  18.4 us
    ppermute x10, waiting for transfers between devices, near(): return lax.ppermute(x, NEAR, [(i, i ^ mask) for i in range(8)])  12.9 us
  transfers between devices with their start and end apart: 46, of which 27 were waited for; matrix products, arithmetic and copies ran while one was open for 7% of the time, Pallas kernels for 0%

profile of v1, /device:TPU:8, one launch (start us, length us, event | category | flops | bytes accessed | tf_op | source)
XLA Modules:
  0.0 433.8 jit_solution(13667983306576835016)
XLA Ops:
  22.5 4.2 collective-permute-done.6
  31.3 51.2 %collective-permute-done.7 = f32[2,1536]{1,0:T(2,128)S(1)} collective-permute-done((f32[2,1536]{1,0:T(2,128)S(1)}, f32[2,1536]{1,0:T(2,128)S(1)}, u32[]{:S(2)}, u32[]{:S(2)}) %collective-permute-start.7) | collective-permute-done | bytes 12320 | tf_op jit(solution)/shard_map/ppermute | solution.py:14
  83.0 65.8 %psum.14 = f32[1024]{0:T(1024)S(1)} all-reduce(f32[1024]{0:T(1024)S(1)} %convert_reduce_fusion), channel_id=1, replica_groups=mesh['y'=4,'xlo'=2,'xhi'=2,'z'=8,'core'=2] {'y','z'}, use_global_device_ids=true, to_apply=%region_1.2 | all-reduce | flops 1024 | bytes 8192 | tf_op jit(solution)/shard_map/psum | solution.py:75
  149.0 69.6 %psum.15 = f32[1024]{0:T(1024)S(1)} all-reduce(f32[1024]{0:T(1024)S(1)} %fusion.11), channel_id=1, replica_groups=mesh['y'=4,'xlo'=2,'xhi'=2,'z'=8,'core'=2] {'y','z'}, use_global_device_ids=true, to_apply=%region_3.4 | all-reduce | flops 1024 | bytes 8192 | tf_op jit(solution)/shard_map/psum | solution.py:77
  220.0 4.2 fusion.8
  231.5 14.8 %collective-permute-start.28 = (bf16[128,768]{1,0:T(8,128)(2,1)S(1)}, bf16[128,768]{1,0:T(8,128)(2,1)S(1)}, u32[]{:S(2)}, u32[]{:S(2)}) collective-permute-start(bf16[128,768]{1,0:T(8,128)(2,1)S(1)} %get-tuple-element.36), channel_id=1, source_target_pairs={{0,128},{64,192},{128,0},{192,64},{1,129},{65,193},{129,1},{193,65... | collective-permute-start | bytes 589832 | tf_op jit(solution)/shard_map/ppermute | solution.py:18
  246.2 3.1 fusion.60
  249.3 3.1 fusion.58
  253.0 3.2 add_convert_fusion
  258.8 3.2 collective-permute-start.11
  262.3 4.8 %collective-permute-done.10 = bf16[128,768]{1,0:T(8,128)(2,1)S(1)} collective-permute-done((bf16[128,768]{1,0:T(8,128)(2,1)S(1)}, bf16[128,768]{1,0:T(8,128)(2,1)S(1)}, u32[]{:S(2)}, u32[]{:S(2)}) %collective-permute-start.10) | collective-permute-done | bytes 196640 | tf_op jit(solution)/shard_map/ppermute | solution.py:18
  272.6 3.2 add_convert_fusion.2
  280.6 4.0 collective-permute-done.12
  285.5 4.3 collective-permute-start.35
  289.9 4.0 collective-permute-start.32
  302.2 3.5 collective-permute-done.14
  305.7 5.1 %collective-permute-done.18 = bf16[128,768]{1,0:T(8,128)(2,1)S(1)} collective-permute-done((bf16[128,768]{1,0:T(8,128)(2,1)S(1)}, bf16[128,768]{1,0:T(8,128)(2,1)S(1)}, u32[]{:S(2)}, u32[]{:S(2)}) %collective-permute-start.18) | collective-permute-done | bytes 196640 | tf_op jit(solution)/shard_map/ppermute | solution.py:18
  318.0 3.8 collective-permute-done.36
  327.6 5.1 %convolution_convert_fusion = bf16[512,1536]{1,0:T(8,128)(2,1)} fusion(bf16[512,1536]{1,0:T(8,128)(2,1)S(1)} %constant_dynamic-update-slice_fusion.8, bf16[768,768]{1,0:T(8,128)(2,1)S(1)} %collective-permute-done.26, bf16[768,768]{1,0:T(8,128)(2,1)S(1)} %collective-permute-done.25, bf16[768,768]{1,0:T(8,128)(2,1)} %collective-permute-done.24, ...), kind=kOutput, calls=%fused_computation.13 | convolution fusion | flops 2435579904 | bytes 7864320 | tf_op jit(solution)/shard_map/dot_general | solution.py:105
  337.2 3.4 collective-permute-done.21
  344.8 5.9 %convolution_convert_fusion.1 = bf16[512,1536]{1,0:T(8,128)(2,1)} fusion(bf16[512,1536]{1,0:T(8,128)(2,1)S(1)} %constant_dynamic-update-slice_fusion.12, bf16[768,768]{1,0:T(8,128)(2,1)} %copy-done.7, bf16[768,768]{1,0:T(8,128)(2,1)} %copy-done.6, bf16[768,768]{1,0:T(8,128)(2,1)} %collective-permute-done.24, bf16[768,768]{1,0:T(8,128)(2,1)S(1)} %copy-done.5), kind=kOutput, calls=%fused_computation.14 | convolution fusion | flops 2435579904 | bytes 7864320 | tf_op jit(solution)/shard_map/dot_general | solution.py:105
  350.7 24.2 %reduce-scatter.5.cloned.1.call-done = bf16[64,1536]{1,0:T(8,128)(2,1)} async-done(((bf16[512,1536]{1,0:T(8,128)(2,1)}), bf16[64,1536]{1,0:T(8,128)(2,1)}) %reduce-scatter.5.cloned.1.call-update) | async-done | bytes 196624 | tf_op jit(solution)/shard_map/reduce_scatter | solution.py:106
  374.9 41.4 %reduce-scatter.3.cloned.1.call-done = bf16[64,1536]{1,0:T(8,128)(2,1)} async-done(((bf16[512,1536]{1,0:T(8,128)(2,1)}), bf16[64,1536]{1,0:T(8,128)(2,1)}) %reduce-scatter.3.cloned.1.call-update) | async-done | bytes 196624 | tf_op jit(solution)/shard_map/reduce_scatter | solution.py:106
  417.3 3.1 collective-permute-start.39
  (167 shorter events, 81.7 us)
Async XLA Ops:
  6.5 213.4 %all-gather.5.cloned.1.call-start = ((), (), s32[]{:S(2)}) async-start(), calls=%async_computation.4 | async-start | bytes 3538944 | tf_op jit(solution)/shard_map/all_gather | solution.py:83
  9.3 12.0 %collective-permute-start.2 = (bf16[48,1024]{1,0:T(8,128)(2,1)S(1)}, bf16[48,1024]{1,0:T(8,128)(2,1)S(1)}, u32[]{:S(2)}, u32[]{:S(2)}) collective-permute-start(bf16[48,1024]{1,0:T(8,128)(2,1)S(1)} %select_n.293), channel_id=1, source_target_pairs={{0,17},{1,16},{16,1},{17,0},{32,49},{33,48},{48,33},{49,32},{2,19}... | collective-permute-start | bytes 294920 | tf_op jit(solution)/shard_map/ppermute | solution.py:22
  28.1 191.9 %all-gather.7.cloned.1.call-start = ((), (), s32[]{:S(2)}) async-start(), calls=%async_computation.5 | async-start | bytes 3538944 | tf_op jit(solution)/shard_map/all_gather | solution.py:83
  28.8 346.0 %reduce-scatter.5.cloned.1.call-start = ((), (), s32[]{:S(2)}) async-start(), calls=%async_computation.3 | async-start | bytes 1769472 | tf_op jit(solution)/shard_map/reduce_scatter | solution.py:106
  28.9 189.8 %collective-permute-start.8 = (bf16[1536,768]{1,0:T(8,128)(2,1)}, bf16[1536,768]{1,0:T(8,128)(2,1)S(1)}, u32[]{:S(2)}, u32[]{:S(2)}) collective-permute-start(bf16[1536,768]{1,0:T(8,128)(2,1)} %param.10), channel_id=1, source_target_pairs={{0,32},{32,0},{1,33},{33,1},{2,34},{34,2},{3,35},{35,3},{4,36},{36... | collective-permute-start | bytes 7077896 | tf_op jit(solution)/shard_map/ppermute | solution.py:14
  30.0 52.6 %collective-permute-start.7 = (f32[2,1536]{1,0:T(2,128)S(1)}, f32[2,1536]{1,0:T(2,128)S(1)}, u32[]{:S(2)}, u32[]{:S(2)}) collective-permute-start(f32[2,1536]{1,0:T(2,128)S(1)} %pad_maximum_fusion.5), channel_id=1, source_target_pairs={{0,32},{32,0},{1,33},{33,1},{2,34},{34,2},{3,35},{35,3},{4,36},{36... | collective-permute-start | bytes 36872 | tf_op jit(solution)/shard_map/ppermute | solution.py:14
  31.1 244.6 %collective-permute-start.20 = (f32[768]{0:T(1024)S(1)}, f32[768]{0:T(1024)S(1)}, u32[]{:S(2)}, u32[]{:S(2)}) collective-permute-start(f32[768]{0:T(1024)S(1)} %copy-done.3), channel_id=1, source_target_pairs={{0,1},{1,0},{2,3},{3,2},{4,5},{5,4},{6,7},{7,6},{8,9},{9,8},{10,11... | collective-permute-start | bytes 9224 | tf_op jit(solution)/shard_map/ppermute | solution.py:14
  82.7 148.7 %collective-permute-start.15 = (bf16[1536,768]{1,0:T(8,128)(2,1)}, bf16[1536,768]{1,0:T(8,128)(2,1)}, u32[]{:S(2)}, u32[]{:S(2)}) collective-permute-start(bf16[1536,768]{1,0:T(8,128)(2,1)} %param.10), channel_id=1, source_target_pairs={{0,1},{1,0},{2,3},{3,2},{4,5},{5,4},{6,7},{7,6},{8,9},{9,8},{10,11... | collective-permute-start | bytes 7077896 | tf_op jit(solution)/shard_map/ppermute | solution.py:14
  218.7 66.2 %collective-permute-start.24 = (bf16[768,768]{1,0:T(8,128)(2,1)}, bf16[768,768]{1,0:T(8,128)(2,1)}, u32[]{:S(2)}, u32[]{:S(2)}) collective-permute-start(bf16[768,768]{1,0:T(8,128)(2,1)} %param.12), channel_id=1, source_target_pairs={{0,32},{32,0},{1,33},{33,1},{2,34},{34,2},{3,35},{35,3},{4,36},{36... | collective-permute-start | bytes 3538952 | tf_op jit(solution)/shard_map/ppermute | solution.py:14
  219.7 32.7 %collective-permute-start.16 = (bf16[1536,768]{1,0:T(8,128)(2,1)S(1)}, bf16[1536,768]{1,0:T(8,128)(2,1)}, u32[]{:S(2)}, u32[]{:S(2)}) collective-permute-start(bf16[1536,768]{1,0:T(8,128)(2,1)S(1)} %collective-permute-done.8), channel_id=1, source_target_pairs={{0,1},{1,0},{2,3},{3,2},{4,5},{5,4},{6,7},{7,6},{8,9},{9,8},{10,11... | collective-permute-start | bytes 7077896 | tf_op jit(solution)/shard_map/ppermute | solution.py:14
  229.3 28.5 %collective-permute-start.27 = (bf16[128,768]{1,0:T(8,128)(2,1)S(1)}, bf16[128,768]{1,0:T(8,128)(2,1)S(1)}, u32[]{:S(2)}, u32[]{:S(2)}) collective-permute-start(bf16[128,768]{1,0:T(8,128)(2,1)S(1)} %get-tuple-element.34), channel_id=1, source_target_pairs={{0,64},{64,128},{128,192},{192,0},{1,65},{65,129},{129,193},{193,1... | collective-permute-start | bytes 589832 | tf_op jit(solution)/shard_map/ppermute | solution.py:18
  231.5 27.3 %collective-permute-start.28 = (bf16[128,768]{1,0:T(8,128)(2,1)S(1)}, bf16[128,768]{1,0:T(8,128)(2,1)S(1)}, u32[]{:S(2)}, u32[]{:S(2)}) collective-permute-start(bf16[128,768]{1,0:T(8,128)(2,1)S(1)} %get-tuple-element.36), channel_id=1, source_target_pairs={{0,128},{64,192},{128,0},{192,64},{1,129},{65,193},{129,1},{193,65... | collective-permute-start | bytes 589832 | tf_op jit(solution)/shard_map/ppermute | solution.py:18
  258.8 10.7 %collective-permute-start.11 = (bf16[128,768]{1,0:T(8,128)(2,1)S(1)}, bf16[128,768]{1,0:T(8,128)(2,1)S(1)}, u32[]{:S(2)}, u32[]{:S(2)}) collective-permute-start(bf16[128,768]{1,0:T(8,128)(2,1)S(1)} %get-tuple-element.27), channel_id=1, source_target_pairs={{0,192},{64,0},{128,64},{192,128},{1,193},{65,1},{129,65},{193,129... | collective-permute-start | bytes 589832 | tf_op jit(solution)/shard_map/ppermute | solution.py:18
  262.0 10.0 %collective-permute-start.9 = (bf16[128,768]{1,0:T(8,128)(2,1)S(1)}, bf16[128,768]{1,0:T(8,128)(2,1)S(1)}, u32[]{:S(2)}, u32[]{:S(2)}) collective-permute-start(bf16[128,768]{1,0:T(8,128)(2,1)S(1)} %get-tuple-element.26), channel_id=1, source_target_pairs={{0,64},{64,128},{128,192},{192,0},{1,65},{65,129},{129,193},{193,1... | collective-permute-start | bytes 589832 | tf_op jit(solution)/shard_map/ppermute | solution.py:18
  267.2 17.8 %collective-permute-start.33 = (bf16[128,768]{1,0:T(8,128)(2,1)S(1)}, bf16[128,768]{1,0:T(8,128)(2,1)S(1)}, u32[]{:S(2)}, u32[]{:S(2)}) collective-permute-start(bf16[128,768]{1,0:T(8,128)(2,1)S(1)} %get-tuple-element.31), channel_id=1, source_target_pairs={{0,64},{64,128},{128,192},{192,0},{1,65},{65,129},{129,193},{193,1... | collective-permute-start | bytes 589832 | tf_op jit(solution)/shard_map/ppermute | solution.py:18
  269.4 11.0 %collective-permute-start.30 = (bf16[128,768]{1,0:T(8,128)(2,1)S(1)}, bf16[128,768]{1,0:T(8,128)(2,1)S(1)}, u32[]{:S(2)}, u32[]{:S(2)}) collective-permute-start(bf16[128,768]{1,0:T(8,128)(2,1)S(1)} %get-tuple-element.18), channel_id=1, source_target_pairs={{0,64},{64,128},{128,192},{192,0},{1,65},{65,129},{129,193},{193,1... | collective-permute-start | bytes 589832 | tf_op jit(solution)/shard_map/ppermute | solution.py:18
  272.4 12.3 %collective-permute-start.12 = (bf16[128,768]{1,0:T(8,128)(2,1)S(1)}, bf16[128,768]{1,0:T(8,128)(2,1)S(1)}, u32[]{:S(2)}, u32[]{:S(2)}) collective-permute-start(bf16[128,768]{1,0:T(8,128)(2,1)S(1)} %get-tuple-element.14), channel_id=1, source_target_pairs={{0,64},{64,128},{128,192},{192,0},{1,65},{65,129},{129,193},{193,1... | collective-permute-start | bytes 589832 | tf_op jit(solution)/shard_map/ppermute | solution.py:18
  284.9 40.6 %collective-permute-start.25 = (bf16[768,768]{1,0:T(8,128)(2,1)S(1)}, bf16[768,768]{1,0:T(8,128)(2,1)S(1)}, u32[]{:S(2)}, u32[]{:S(2)}) collective-permute-start(bf16[768,768]{1,0:T(8,128)(2,1)S(1)} %copy-done.5), channel_id=1, source_target_pairs={{0,1},{1,0},{2,3},{3,2},{4,5},{5,4},{6,7},{7,6},{8,9},{9,8},{10,11... | collective-permute-start | bytes 3538952 | tf_op jit(solution)/shard_map/ppermute | solution.py:14
  285.0 40.5 %collective-permute-start.26 = (bf16[768,768]{1,0:T(8,128)(2,1)}, bf16[768,768]{1,0:T(8,128)(2,1)S(1)}, u32[]{:S(2)}, u32[]{:S(2)}) collective-permute-start(bf16[768,768]{1,0:T(8,128)(2,1)} %collective-permute-done.24), channel_id=1, source_target_pairs={{0,1},{1,0},{2,3},{3,2},{4,5},{5,4},{6,7},{7,6},{8,9},{9,8},{10,11... | collective-permute-start | bytes 3538952 | tf_op jit(solution)/shard_map/ppermute | solution.py:14
  285.5 11.8 %collective-permute-start.35 = (bf16[128,768]{1,0:T(8,128)(2,1)S(1)}, bf16[128,768]{1,0:T(8,128)(2,1)S(1)}, u32[]{:S(2)}, u32[]{:S(2)}) collective-permute-start(bf16[128,768]{1,0:T(8,128)(2,1)S(1)} %get-tuple-element.32), channel_id=1, source_target_pairs={{0,192},{64,0},{128,64},{192,128},{1,193},{65,1},{129,65},{193,129... | collective-permute-start | bytes 589832 | tf_op jit(solution)/shard_map/ppermute | solution.py:18
  289.9 11.6 %collective-permute-start.32 = (bf16[128,768]{1,0:T(8,128)(2,1)S(1)}, bf16[128,768]{1,0:T(8,128)(2,1)S(1)}, u32[]{:S(2)}, u32[]{:S(2)}) collective-permute-start(bf16[128,768]{1,0:T(8,128)(2,1)S(1)} %get-tuple-element.18), channel_id=1, source_target_pairs={{0,192},{64,0},{128,64},{192,128},{1,193},{65,1},{129,65},{193,129... | collective-permute-start | bytes 589832 | tf_op jit(solution)/shard_map/ppermute | solution.py:18
  294.0 11.6 %collective-permute-start.14 = (bf16[128,768]{1,0:T(8,128)(2,1)S(1)}, bf16[128,768]{1,0:T(8,128)(2,1)S(1)}, u32[]{:S(2)}, u32[]{:S(2)}) collective-permute-start(bf16[128,768]{1,0:T(8,128)(2,1)S(1)} %get-tuple-element.14), channel_id=1, source_target_pairs={{0,192},{64,0},{128,64},{192,128},{1,193},{65,1},{129,65},{193,129... | collective-permute-start | bytes 589832 | tf_op jit(solution)/shard_map/ppermute | solution.py:18
  315.6 9.9 %collective-permute-start.38 = (bf16[128,768]{1,0:T(8,128)(2,1)S(1)}, bf16[128,768]{1,0:T(8,128)(2,1)S(1)}, u32[]{:S(2)}, u32[]{:S(2)}) collective-permute-start(bf16[128,768]{1,0:T(8,128)(2,1)S(1)} %get-tuple-element.66), channel_id=1, source_target_pairs={{0,192},{64,0},{128,64},{192,128},{1,193},{65,1},{129,65},{193,129... | collective-permute-start | bytes 589832 | tf_op jit(solution)/shard_map/ppermute | solution.py:18
  332.7 83.6 %reduce-scatter.3.cloned.1.call-start = ((), (), s32[]{:S(2)}) async-start(), calls=%async_computation.2 | async-start | bytes 1769472 | tf_op jit(solution)/shard_map/reduce_scatter | solution.py:106
  (30 other events, 272.2 us)
Sparse Core Ops, SparseCore 0:
  28.2 46.6 all-gather.4
  76.6 44.3 all-gather.6
  332.8 42.0 reduce-scatter.4
  377.3 38.9 reduce-scatter.2

commit v2 on v1

v2 whole, which is shorter than its diff:
```python
import jax
import jax.numpy as jnp
from jax import lax
from jax.sharding import Mesh, PartitionSpec as P

f32, bf16 = jnp.float32, jnp.bfloat16
NY, NXLO, NXHI, NZ, NCORE = 4, 2, 2, 8, 2
SEC = ("y", "xlo")
DEV = ("xhi", "z", "core")
NEAR = ("xlo", "xhi", "core")


def swap(x, axis):
    return lax.ppermute(x, axis, [(0, 1), (1, 0)])


def shift(x, axis, d):
    n = lax.axis_size(axis)
    return lax.ppermute(x, axis, [(i, (i + d) % n) for i in range(n)])


def near(x, mask):
    return lax.ppermute(x, NEAR, [(i, i ^ mask) for i in range(8)])


def ordered(which, own, other):
    first = which == 0
    return jnp.where(first, own, other), jnp.where(first, other, own)


def ring_sum(down, z):
    rows, cols = down.shape[0] // NZ, down.shape[1]
    half = cols // 2

    def block(d):
        return lax.dynamic_slice_in_dim(down, (z + d) % NZ * rows, rows, 0)

    def add(a, b):
        return (a.astype(f32) + b.astype(f32)).astype(bf16)

    opposite = block(NZ // 2)
    up = shift(opposite[:, :half], "z", 1)
    dn = shift(opposite[:, half:], "z", -1)
    for d in range(NZ // 2 - 1, 0, -1):
        a, b = block(d), block(-d)
        if d == NZ // 2 - 1:
            a = jnp.concatenate([add(a[:, :half], up), a[:, half:]], axis=1)
            b = jnp.concatenate([b[:, :half], add(b[:, half:], dn)], axis=1)
        else:
            a, b = add(a, up), add(b, dn)
        up, dn = shift(a, "z", 1), shift(b, "z", -1)
    return block(0).astype(f32) + up.astype(f32) + dn.astype(f32)


def local(acts, ln_gain, ln_bias, w1, up_bias, w2, down_bias):
    micros, seq, width = acts.shape
    own_seq = seq // (NXHI * NZ * NCORE)
    chunk = NZ * own_seq
    tokens = NXHI * chunk
    y, xlo, xhi, z, core = (lax.axis_index(a) for a in ("y", "xlo", "xhi", "z", "core"))
    features = width * 256
    group = features // NY

    tiles = acts.reshape(micros, NXHI, NZ, NCORE, own_seq, width)
    tiles = tiles.transpose(0, 3, 5, 1, 2, 4).reshape(micros, NCORE, width, tokens)
    mine, theirs = ordered(xlo, tiles[0], tiles[1])
    quarter = [ordered(core, part[0], part[1]) for part in (mine, theirs)]

    def arrived(rx, rh, rc):
        piece, mask = quarter[rx][rc], rx * 4 + rh * 2 + rc
        return near(piece, mask) if mask else piece

    rows = []
    for rx in range(2):
        by_hi = []
        for rh in range(2):
            a, b = ordered(core, arrived(rx, rh, 0), arrived(rx, rh, 1))
            by_hi.append(jnp.concatenate([a, b], axis=0))
        rows.append(jnp.stack(ordered(xhi, *by_hi)))
    x = jnp.stack(rows)

    k1, n1 = w1.shape
    scaled = (w1.astype(f32) * ln_gain[:, None]).astype(bf16)
    col = jnp.sum(scaled.astype(f32), axis=0)
    shiftv = jnp.sum(w1.astype(f32) * ln_bias[:, None], axis=0)
    vec = jnp.stack([col, shiftv])
    vec = vec + swap(vec, "xlo")
    vec = jnp.stack([vec, swap(vec, "core")])
    vecs = [vec] + [shift(vec, "y", d) for d in range(1, NY)]
    offset = sum(v[:, 1] for v in vecs) + jnp.stack([up_bias, swap(up_bias, "core")])

    scaled = scaled.reshape(NXHI, NZ, 2 * width, n1).transpose(1, 0, 2, 3).reshape(k1, n1)
    x, vec, scaled = lax.optimization_barrier((x, vec, scaled))
    w1s = [[scaled, swap(scaled, "core")]]
    far = swap(scaled, "xlo")
    w1s.append([far, swap(far, "core")])
    far, w2 = lax.optimization_barrier((far, w2))
    far2 = swap(w2, "xlo")
    w2_cat = jnp.concatenate(
        [
            jnp.concatenate([w2, far2], axis=1),
            jnp.concatenate([swap(w2, "core"), swap(far2, "core")], axis=1),
        ],
        axis=0,
    )

    outs = []
    for t in range(NXHI):
        gathered = lax.all_gather(x[..., t * chunk : (t + 1) * chunk], "z")
        part = chunk // NY
        g32 = gathered.astype(f32)
        mean = jnp.sum(g32, axis=(0, 1, 2, 3)) / group
        dev = g32 - mean
        stats = jnp.stack([mean, jnp.sum(dev * dev, axis=(0, 1, 2, 3))])
        ups = []
        for j in range(NCORE):
            acc = sum(
                lax.dot_general(
                    gathered[:, r].reshape(k1, chunk),
                    w1s[r][j],
                    (((0,), (0,)), ((), ())),
                    preferred_element_type=f32,
                )
                for r in range(NXLO)
            )
            ups.append((acc - mean[:, None] * vec[j, 0][None, :]).astype(bf16))

        def block(d):
            at = (y + d) % NY * part
            return jnp.concatenate(
                [lax.dynamic_slice_in_dim(up, at, part, 0) for up in ups], axis=1
            )

        def own_stats(d):
            return lax.dynamic_slice_in_dim(stats, (y + d) % NY * part, part, 1)

        total = block(0).astype(f32)
        for d in (2, 1, 3):
            total = total + shift(block(d), "y", d).astype(f32)
        every = [own_stats(0)] + [shift(own_stats(d), "y", d) for d in range(1, NY)]
        center = sum(s[0] for s in every) / NY
        spread = sum(s[1] + group * jnp.square(s[0] - center) for s in every) / features
        for s, v in zip(every, vecs):
            total = total + (s[0] - center)[:, None] * v[:, 0].reshape(1, -1)
        total = total * lax.rsqrt(spread + 1e-05)[:, None] + offset.reshape(1, -1)
        act = jax.nn.gelu(total, approximate=True).astype(bf16)
        hidden = jnp.zeros((chunk, NCORE * n1), bf16)
        for d in range(NY):
            got = shift(act, "y", d) if d else act
            hidden = lax.dynamic_update_slice_in_dim(hidden, got, (y - d) % NY * part, 0)
        down = jnp.dot(hidden, w2_cat, preferred_element_type=f32).astype(bf16)
        outs.append(ring_sum(down, z).astype(bf16))

    keep, send = ordered(xhi, outs[0], outs[1])
    cols = down_bias.shape[0]
    here = keep[:, :cols].astype(f32) + near(send[:, :cols], 2).astype(f32)
    other = near(keep[:, cols:], 4).astype(f32) + near(send[:, cols:], 6).astype(f32)
    both = jnp.stack(ordered(xlo, here, other))
    return (both + down_bias).astype(bf16)


def solution(mesh):
    fine = Mesh(mesh.devices.reshape(NY, NXLO, NXHI, NZ, NCORE), SEC + DEV)
    in_specs = (
        P(None, None, SEC + DEV),
        P(SEC),
        P(SEC),
        P(SEC, DEV),
        P(DEV),
        P(DEV, SEC),
        P(SEC),
    )
    return jax.shard_map(
        local, mesh=fine, in_specs=in_specs, out_specs=P(None, DEV, SEC), check_vma=False
    )
```

time: 442 us -> 313 us (0.71)
  blocking collectives: 135 us -> 0 us
  starting transfers between devices: 64.6 us -> 84.9 us
  waiting for transfers between devices: 173 us -> 154 us
  other arithmetic: 7.95 us -> 15.3 us
    psum x2 -> x0, blocking collectives: 135 us -> none  [the longest x1 69.6 us: local(): var = lax.psum(jnp.sum(off * off, axis=(0, 1, 2)), ('y', 'z')) / features]
    reduce_scatter x2 -> x0, waiting for transfers between devices: 65.6 us -> none  [local(): outs.append(lax.psum_scatter(down, 'z', scatter_dimension=0, tiled=True))]
    all_gather x2, waiting for transfers between devices: 0.04 us -> 32.3 us  [local(): gathered = lax.all_gather(x[..., t * chunk:(t + 1) * chunk], 'z')]
    ppermute x24 -> x37, waiting for transfers between devices: 42.3 us -> 64.6 us  [shift(): return lax.ppermute(x, axis, [(i, (i + d) % n) for i in range(n)])]
    ppermute x24 -> x37, starting transfers between devices: 47.6 us -> 68.1 us  [shift(): return lax.ppermute(x, axis, [(i, (i + d) % n) for i in range(n)])]
    reduce_sum x2 -> x5, other arithmetic: 0.38 us -> 10.1 us  [the longest x2 5.04 us: local(): mean = jnp.sum(g32, axis=(0, 1, 2, 3)) / group]
    ppermute x8 -> x9, waiting for transfers between devices: 51.2 us -> 45.4 us  [swap(): return lax.ppermute(x, axis, [(0, 1), (1, 0)])]
  transfers between devices with their start and end apart: 46 -> 58, of which waited for: 27 -> 26; matrix products, arithmetic and copies ran while one was open for 7% -> 16% of each run, Pallas kernels for 0% -> 0%
where the time goes in v2:
time: 313 us; the launch traced here: 307 us
  waiting for transfers between devices  154 us (49%)
  starting transfers between devices  84.9 us (27%)
  matrix products  29.6 us (9%)
  other arithmetic  15.3 us (5%)
  between operations  14.5 us (5%)
  local copies, waits for them, and re-layouts  9.67 us (3%)
    ppermute x37, starting transfers between devices, shift(): return lax.ppermute(x, axis, [(i, (i + d) % n) for i in range(n)])  68.1 us
    ppermute x37, waiting for transfers between devices, shift(): return lax.ppermute(x, axis, [(i, (i + d) % n) for i in range(n)])  64.6 us
    ppermute x9, waiting for transfers between devices, swap(): return lax.ppermute(x, axis, [(0, 1), (1, 0)])  45.4 us
    all_gather x2, waiting for transfers between devices, local(): gathered = lax.all_gather(x[..., t * chunk:(t + 1) * chunk], 'z')  32.3 us
    dot_general x8, matrix products, local(): lax.dot_general(gathered[:, r].reshape(k1, chunk), w1s[r][j], (((0,), (0,...  21.8 us
    ppermute x10, starting transfers between devices, near(): return lax.ppermute(x, NEAR, [(i, i ^ mask) for i in range(8)])  12.9 us
    ppermute x10, waiting for transfers between devices, near(): return lax.ppermute(x, NEAR, [(i, i ^ mask) for i in range(8)])  10.4 us
    dot_general x2, matrix products, local(): down = jnp.dot(hidden, w2_cat, preferred_element_type=f32).astype(bf16)  7.75 us
  transfers between devices with their start and end apart: 58, of which 26 were waited for; matrix products, arithmetic and copies ran while one was open for 16% of the time, Pallas kernels for 0%

profile of v2, /device:TPU:8, one launch (start us, length us, event | category | flops | bytes accessed | tf_op | source)
XLA Modules:
  0.0 307.5 jit_solution(8403095874003067450)
XLA Ops:
  12.5 3.3 %convert_reduce_fusion.2 = (f32[768]{0:T(1024)S(1)}, bf16[1536,768]{1,0:T(8,128)(2,1)}, f32[768]{0:T(1024)S(1)}) fusion(f32[1536]{0:T(1024)S(1)} %copy-done.5, bf16[1536,768]{1,0:T(8,128)(2,1)} %param.10, f32[1536]{0:T(1024)S(1)} %copy-done.6), kind=kLoop, calls=%fused_computation.13 | loop fusion | flops 8256000 | bytes 4737024 | tf_op jit(solution)/shard_map/reduce_sum | solution.py:84
  41.7 43.2 %collective-permute-done.9 = bf16[1536,768]{1,0:T(8,128)(2,1)} collective-permute-done((bf16[1536,768]{1,0:T(8,128)(2,1)S(1)}, bf16[1536,768]{1,0:T(8,128)(2,1)}, u32[]{:S(2)}, u32[]{:S(2)}) %collective-permute-start.9) | collective-permute-done | bytes 2359328 | tf_op jit(solution)/shard_map/ppermute | solution.py:14
  92.3 32.3 %all-gather.7.cloned.1.call-done = bf16[16,2,96,512]{3,2,1,0:T(8,128)(2,1)} async-done(((bf16[2,2,96,512]{3,2,1,0:T(8,128)(2,1)}), bf16[16,2,96,512]{3,2,1,0:T(8,128)(2,1)}) %all-gather.7.cloned.1.call-update) | async-done | bytes 3145744 | tf_op jit(solution)/shard_map/all_gather | solution.py:109
  137.7 3.2 %subtract_convert_fusion.1 = bf16[512,768]{1,0:T(8,128)(2,1)S(1)} fusion(f32[512,768]{1,0:T(8,128)S(1)} %fusion.58, bf16[1536,512]{1,0:T(8,128)(2,1)S(1)} %bitcast.190, bf16[1536,768]{1,0:T(8,128)(2,1)} %collective-permute-done.9, f32[512]{0:T(512)S(1)} %broadcast_multiply_fusion, f32[768]{0:T(1024)S(1)} %get-tuple-element.18), kind=kOutput, calls=%fused_computation.17 | convolution fusion | flops 1209532416 | bytes 6296576 | tf_op jit(solution)/shard_map/dot_general | solution.py:118
  140.9 11.1 %collective-permute-start.17 = (f32[2,128]{1,0:T(2,128)S(1)}, f32[2,128]{1,0:T(2,128)S(1)}, u32[]{:S(2)}, u32[]{:S(2)}) collective-permute-start(f32[2,128]{1,0:T(2,128)S(1)} %get-tuple-element.107), channel_id=1, source_target_pairs={{0,192},{64,0},{128,64},{192,128},{1,193},{65,1},{129,65},{193,129... | collective-permute-start | bytes 3080 | tf_op jit(solution)/shard_map/ppermute | solution.py:19
  155.2 3.2 %subtract_convert_fusion.2 = bf16[512,768]{1,0:T(8,128)(2,1)S(1)} fusion(f32[512,768]{1,0:T(8,128)S(1)} %fusion.57, bf16[1536,512]{1,0:T(8,128)(2,1)S(1)} %bitcast.187, bf16[1536,768]{1,0:T(8,128)(2,1)} %collective-permute-done.11, f32[768]{0:T(1024)S(1)} %get-tuple-element.19, f32[512]{0:T(512)S(1)} %broadcast_multiply_fusion.1), kind=kOutput, calls=%fused_computation.18 | convolution fusion | flops 1209532416 | bytes 6296576 | tf_op jit(solution)/shard_map/dot_general | solution.py:118
  165.1 3.6 %collective-permute-start.40 = (f32[2,128]{1,0:T(2,128)S(1)}, f32[2,128]{1,0:T(2,128)S(1)}, u32[]{:S(2)}, u32[]{:S(2)}) collective-permute-start(f32[2,128]{1,0:T(2,128)S(1)} %get-tuple-element.102), channel_id=1, source_target_pairs={{0,128},{64,192},{128,0},{192,64},{1,129},{65,193},{129,1},{193,65... | collective-permute-start | bytes 3080 | tf_op jit(solution)/shard_map/ppermute | solution.py:19
  173.0 3.9 %collective-permute-done.41 = f32[2,128]{1,0:T(2,128)S(1)} collective-permute-done((f32[2,128]{1,0:T(2,128)S(1)}, f32[2,128]{1,0:T(2,128)S(1)}, u32[]{:S(2)}, u32[]{:S(2)}) %collective-permute-start.41) | collective-permute-done | bytes 1056 | tf_op jit(solution)/shard_map/ppermute | solution.py:19
  176.9 5.4 %collective-permute-done.36 = bf16[128,1536]{1,0:T(8,128)(2,1)S(1)} collective-permute-done((bf16[128,1536]{1,0:T(8,128)(2,1)S(1)}, bf16[128,1536]{1,0:T(8,128)(2,1)S(1)}, u32[]{:S(2)}, u32[]{:S(2)}) %collective-permute-start.36) | collective-permute-done | bytes 393248 | tf_op jit(solution)/shard_map/ppermute | solution.py:19
  183.7 7.6 %collective-permute-done.37 = bf16[128,1536]{1,0:T(8,128)(2,1)S(1)} collective-permute-done((bf16[128,1536]{1,0:T(8,128)(2,1)S(1)}, bf16[128,1536]{1,0:T(8,128)(2,1)S(1)}, u32[]{:S(2)}, u32[]{:S(2)}) %collective-permute-start.37) | collective-permute-done | bytes 393248 | tf_op jit(solution)/shard_map/ppermute | solution.py:19
  194.6 3.3 %collective-permute-done.12 = bf16[128,1536]{1,0:T(8,128)(2,1)S(1)} collective-permute-done((bf16[128,1536]{1,0:T(8,128)(2,1)S(1)}, bf16[128,1536]{1,0:T(8,128)(2,1)S(1)}, u32[]{:S(2)}, u32[]{:S(2)}) %collective-permute-start.12) | collective-permute-done | bytes 393248 | tf_op jit(solution)/shard_map/ppermute | solution.py:19
  198.5 9.6 %collective-permute-done.13 = bf16[128,1536]{1,0:T(8,128)(2,1)S(1)} collective-permute-done((bf16[128,1536]{1,0:T(8,128)(2,1)S(1)}, bf16[128,1536]{1,0:T(8,128)(2,1)S(1)}, u32[]{:S(2)}, u32[]{:S(2)}) %collective-permute-start.13) | collective-permute-done | bytes 393248 | tf_op jit(solution)/shard_map/ppermute | solution.py:19
  208.6 3.8 %collective-permute-start.44 = (bf16[128,1536]{1,0:T(8,128)(2,1)S(1)}, bf16[128,1536]{1,0:T(8,128)(2,1)S(1)}, u32[]{:S(2)}, u32[]{:S(2)}) collective-permute-start(bf16[128,1536]{1,0:T(8,128)(2,1)S(1)} %get-tuple-element.31), channel_id=1, source_target_pairs={{0,192},{64,0},{128,64},{192,128},{1,193},{65,1},{129,65},{193,129... | collective-permute-start | bytes 1179656 | tf_op jit(solution)/shard_map/ppermute | solution.py:19
  213.4 8.6 %collective-permute-done.42 = bf16[128,1536]{1,0:T(8,128)(2,1)S(1)} collective-permute-done((bf16[128,1536]{1,0:T(8,128)(2,1)S(1)}, bf16[128,1536]{1,0:T(8,128)(2,1)S(1)}, u32[]{:S(2)}, u32[]{:S(2)}) %collective-permute-start.42) | collective-permute-done | bytes 393248 | tf_op jit(solution)/shard_map/ppermute | solution.py:19
  225.8 3.9 %convolution_convert_fusion = bf16[512,1536]{1,0:T(8,128)(2,1)S(1)} fusion(bf16[512,1536]{1,0:T(8,128)(2,1)S(1)} %constant_dynamic-update-slice_fusion, bf16[768,768]{1,0:T(8,128)(2,1)S(1)} %collective-permute-done.27, bf16[768,768]{1,0:T(8,128)(2,1)S(1)} %collective-permute-done.26, bf16[768,768]{1,0:T(8,128)(2,1)} %collective-permute-done.25, ...), kind=kOutput, calls=%fused_computation.14 | convolution fusion | flops 2435579904 | bytes 7864320 | tf_op jit(solution)/shard_map/dot_general | solution.py:151
  229.8 3.2 %collective-permute-start.49 = (bf16[64,768]{1,0:T(8,128)(2,1)S(1)}, bf16[64,768]{1,0:T(8,128)(2,1)S(1)}, u32[]{:S(2)}, u32[]{:S(2)}) collective-permute-start(bf16[64,768]{1,0:T(8,128)(2,1)S(1)} %get-tuple-element.50), channel_id=1, source_target_pairs={{0,14},{2,0},{4,2},{6,4},{8,6},{10,8},{12,10},{14,12},{1,15},{3,1}... | collective-permute-start | bytes 294920 | tf_op jit(solution)/shard_map/ppermute | solution.py:19
  233.0 9.8 %collective-permute-done.22 = bf16[128,1536]{1,0:T(8,128)(2,1)S(1)} collective-permute-done((bf16[128,1536]{1,0:T(8,128)(2,1)S(1)}, bf16[128,1536]{1,0:T(8,128)(2,1)S(1)}, u32[]{:S(2)}, u32[]{:S(2)}) %collective-permute-start.22) | collective-permute-done | bytes 393248 | tf_op jit(solution)/shard_map/ppermute | solution.py:19
  243.0 3.9 %convolution_convert_fusion.1 = bf16[512,1536]{1,0:T(8,128)(2,1)S(1)} fusion(bf16[512,1536]{1,0:T(8,128)(2,1)S(1)} %constant_dynamic-update-slice_fusion.4, bf16[768,768]{1,0:T(8,128)(2,1)S(1)} %collective-permute-done.27, bf16[768,768]{1,0:T(8,128)(2,1)S(1)} %collective-permute-done.26, bf16[768,768]{1,0:T(8,128)(2,1)} %collective-permute-done.25, ...), kind=kOutput, calls=%fused_computation.15 | convolution fusion | flops 2435579904 | bytes 7864320 | tf_op jit(solution)/shard_map/dot_general | solution.py:151
  247.2 3.2 %collective-permute-start.32 = (bf16[64,768]{1,0:T(8,128)(2,1)S(1)}, bf16[64,768]{1,0:T(8,128)(2,1)S(1)}, u32[]{:S(2)}, u32[]{:S(2)}) collective-permute-start(bf16[64,768]{1,0:T(8,128)(2,1)S(1)} %get-tuple-element.58), channel_id=1, source_target_pairs={{0,14},{2,0},{4,2},{6,4},{8,6},{10,8},{12,10},{14,12},{1,15},{3,1}... | collective-permute-start | bytes 294920 | tf_op jit(solution)/shard_map/ppermute | solution.py:19
  253.7 3.8 %collective-permute-start.33 = (bf16[64,1536]{1,0:T(8,128)(2,1)S(1)}, bf16[64,1536]{1,0:T(8,128)(2,1)S(1)}, u32[]{:S(2)}, u32[]{:S(2)}) collective-permute-start(bf16[64,1536]{1,0:T(8,128)(2,1)S(1)} %pad_maximum_fusion.12), channel_id=1, source_target_pairs={{0,14},{2,0},{4,2},{6,4},{8,6},{10,8},{12,10},{14,12},{1,15},{3,1}... | collective-permute-start | bytes 589832 | tf_op jit(solution)/shard_map/ppermute | solution.py:19
  260.1 5.1 %collective-permute-done.29 = bf16[64,1536]{1,0:T(8,128)(2,1)S(1)} collective-permute-done((bf16[64,1536]{1,0:T(8,128)(2,1)S(1)}, bf16[64,1536]{1,0:T(8,128)(2,1)S(1)}, u32[]{:S(2)}, u32[]{:S(2)}) %collective-permute-start.29) | collective-permute-done | bytes 196640 | tf_op jit(solution)/shard_map/ppermute | solution.py:19
  265.5 3.9 %collective-permute-done.47 = bf16[64,1536]{1,0:T(8,128)(2,1)S(1)} collective-permute-done((bf16[64,1536]{1,0:T(8,128)(2,1)S(1)}, bf16[64,1536]{1,0:T(8,128)(2,1)S(1)}, u32[]{:S(2)}, u32[]{:S(2)}) %collective-permute-start.47) | collective-permute-done | bytes 196640 | tf_op jit(solution)/shard_map/ppermute | solution.py:19
  278.0 3.8 %collective-permute-start.52 = (bf16[64,1536]{1,0:T(8,128)(2,1)S(1)}, bf16[64,1536]{1,0:T(8,128)(2,1)S(1)}, u32[]{:S(2)}, u32[]{:S(2)}) collective-permute-start(bf16[64,1536]{1,0:T(8,128)(2,1)S(1)} %add_convert_fusion.1), channel_id=1, source_target_pairs={{0,14},{2,0},{4,2},{6,4},{8,6},{10,8},{12,10},{14,12},{1,15},{3,1}... | collective-permute-start | bytes 589832 | tf_op jit(solution)/shard_map/ppermute | solution.py:19
  281.8 3.7 %collective-permute-start.35 = (bf16[64,1536]{1,0:T(8,128)(2,1)S(1)}, bf16[64,1536]{1,0:T(8,128)(2,1)S(1)}, u32[]{:S(2)}, u32[]{:S(2)}) collective-permute-start(bf16[64,1536]{1,0:T(8,128)(2,1)S(1)} %add_convert_fusion.6), channel_id=1, source_target_pairs={{0,14},{2,0},{4,2},{6,4},{8,6},{10,8},{12,10},{14,12},{1,15},{3,1}... | collective-permute-start | bytes 589832 | tf_op jit(solution)/shard_map/ppermute | solution.py:19
  (214 shorter events, 106.7 us)
Async XLA Ops:
  6.5 80.2 %all-gather.5.cloned.1.call-start = ((), (), s32[]{:S(2)}) async-start(), calls=%async_computation | async-start | bytes 3538944 | tf_op jit(solution)/shard_map/all_gather | solution.py:109
  32.1 92.5 %all-gather.7.cloned.1.call-start = ((), (), s32[]{:S(2)}) async-start(), calls=%async_computation.1 | async-start | bytes 3538944 | tf_op jit(solution)/shard_map/all_gather | solution.py:109
  32.9 52.1 %collective-permute-start.9 = (bf16[1536,768]{1,0:T(8,128)(2,1)S(1)}, bf16[1536,768]{1,0:T(8,128)(2,1)}, u32[]{:S(2)}, u32[]{:S(2)}) collective-permute-start(bf16[1536,768]{1,0:T(8,128)(2,1)S(1)} %bitcast.182), channel_id=1, source_target_pairs={{0,32},{32,0},{1,33},{33,1},{2,34},{34,2},{3,35},{35,3},{4,36},{36... | collective-permute-start | bytes 7077896 | tf_op jit(solution)/shard_map/ppermute | solution.py:14
  41.6 99.3 %collective-permute-start.10 = (bf16[1536,768]{1,0:T(8,128)(2,1)S(1)}, bf16[1536,768]{1,0:T(8,128)(2,1)}, u32[]{:S(2)}, u32[]{:S(2)}) collective-permute-start(bf16[1536,768]{1,0:T(8,128)(2,1)S(1)} %bitcast.183), channel_id=1, source_target_pairs={{0,1},{1,0},{2,3},{3,2},{4,5},{5,4},{6,7},{7,6},{8,9},{9,8},{10,11... | collective-permute-start | bytes 7077896 | tf_op jit(solution)/shard_map/ppermute | solution.py:14
  85.0 80.1 %collective-permute-start.25 = (bf16[768,768]{1,0:T(8,128)(2,1)}, bf16[768,768]{1,0:T(8,128)(2,1)}, u32[]{:S(2)}, u32[]{:S(2)}) collective-permute-start(bf16[768,768]{1,0:T(8,128)(2,1)} %param.12), channel_id=1, source_target_pairs={{0,32},{32,0},{1,33},{33,1},{2,34},{34,2},{3,35},{35,3},{4,36},{36... | collective-permute-start | bytes 3538952 | tf_op jit(solution)/shard_map/ppermute | solution.py:14
  86.7 68.4 %collective-permute-start.11 = (bf16[1536,768]{1,0:T(8,128)(2,1)}, bf16[1536,768]{1,0:T(8,128)(2,1)}, u32[]{:S(2)}, u32[]{:S(2)}) collective-permute-start(bf16[1536,768]{1,0:T(8,128)(2,1)} %collective-permute-done.9), channel_id=1, source_target_pairs={{0,1},{1,0},{2,3},{3,2},{4,5},{5,4},{6,7},{7,6},{8,9},{9,8},{10,11... | collective-permute-start | bytes 7077896 | tf_op jit(solution)/shard_map/ppermute | solution.py:14
  128.5 40.2 %collective-permute-start.15 = (f32[2,128]{1,0:T(2,128)S(1)}, f32[2,128]{1,0:T(2,128)S(1)}, u32[]{:S(2)}, u32[]{:S(2)}) collective-permute-start(f32[2,128]{1,0:T(2,128)S(1)} %get-tuple-element.105), channel_id=1, source_target_pairs={{0,64},{64,128},{128,192},{192,0},{1,65},{65,129},{129,193},{193,1... | collective-permute-start | bytes 3080 | tf_op jit(solution)/shard_map/ppermute | solution.py:19
  130.0 38.7 %collective-permute-start.16 = (f32[2,128]{1,0:T(2,128)S(1)}, f32[2,128]{1,0:T(2,128)S(1)}, u32[]{:S(2)}, u32[]{:S(2)}) collective-permute-start(f32[2,128]{1,0:T(2,128)S(1)} %get-tuple-element.106), channel_id=1, source_target_pairs={{0,128},{64,192},{128,0},{192,64},{1,129},{65,193},{129,1},{193,65... | collective-permute-start | bytes 3080 | tf_op jit(solution)/shard_map/ppermute | solution.py:19
  140.9 29.2 %collective-permute-start.17 = (f32[2,128]{1,0:T(2,128)S(1)}, f32[2,128]{1,0:T(2,128)S(1)}, u32[]{:S(2)}, u32[]{:S(2)}) collective-permute-start(f32[2,128]{1,0:T(2,128)S(1)} %get-tuple-element.107), channel_id=1, source_target_pairs={{0,192},{64,0},{128,64},{192,128},{1,193},{65,1},{129,65},{193,129... | collective-permute-start | bytes 3080 | tf_op jit(solution)/shard_map/ppermute | solution.py:19
  155.1 16.3 %collective-permute-start.39 = (f32[2,128]{1,0:T(2,128)S(1)}, f32[2,128]{1,0:T(2,128)S(1)}, u32[]{:S(2)}, u32[]{:S(2)}) collective-permute-start(f32[2,128]{1,0:T(2,128)S(1)} %get-tuple-element.101), channel_id=1, source_target_pairs={{0,64},{64,128},{128,192},{192,0},{1,65},{65,129},{129,193},{193,1... | collective-permute-start | bytes 3080 | tf_op jit(solution)/shard_map/ppermute | solution.py:19
  170.1 21.1 %collective-permute-start.37 = (bf16[128,1536]{1,0:T(8,128)(2,1)S(1)}, bf16[128,1536]{1,0:T(8,128)(2,1)S(1)}, u32[]{:S(2)}, u32[]{:S(2)}) collective-permute-start(bf16[128,1536]{1,0:T(8,128)(2,1)S(1)} %pad_maximum_fusion.5), channel_id=1, source_target_pairs={{0,64},{64,128},{128,192},{192,0},{1,65},{65,129},{129,193},{193,1... | collective-permute-start | bytes 1179656 | tf_op jit(solution)/shard_map/ppermute | solution.py:19
  171.4 19.8 %collective-permute-start.38 = (bf16[128,1536]{1,0:T(8,128)(2,1)S(1)}, bf16[128,1536]{1,0:T(8,128)(2,1)S(1)}, u32[]{:S(2)}, u32[]{:S(2)}) collective-permute-start(bf16[128,1536]{1,0:T(8,128)(2,1)S(1)} %pad_maximum_fusion.6), channel_id=1, source_target_pairs={{0,192},{64,0},{128,64},{192,128},{1,193},{65,1},{129,65},{193,129... | collective-permute-start | bytes 1179656 | tf_op jit(solution)/shard_map/ppermute | solution.py:19
  172.9 52.8 %collective-permute-start.26 = (bf16[768,768]{1,0:T(8,128)(2,1)S(1)}, bf16[768,768]{1,0:T(8,128)(2,1)S(1)}, u32[]{:S(2)}, u32[]{:S(2)}) collective-permute-start(bf16[768,768]{1,0:T(8,128)(2,1)S(1)} %copy-done.9), channel_id=1, source_target_pairs={{0,1},{1,0},{2,3},{3,2},{4,5},{5,4},{6,7},{7,6},{8,9},{9,8},{10,11... | collective-permute-start | bytes 3538952 | tf_op jit(solution)/shard_map/ppermute | solution.py:14
  176.9 48.8 %collective-permute-start.27 = (bf16[768,768]{1,0:T(8,128)(2,1)}, bf16[768,768]{1,0:T(8,128)(2,1)S(1)}, u32[]{:S(2)}, u32[]{:S(2)}) collective-permute-start(bf16[768,768]{1,0:T(8,128)(2,1)} %collective-permute-done.25), channel_id=1, source_target_pairs={{0,1},{1,0},{2,3},{3,2},{4,5},{5,4},{6,7},{7,6},{8,9},{9,8},{10,11... | collective-permute-start | bytes 3538952 | tf_op jit(solution)/shard_map/ppermute | solution.py:14
  191.2 16.9 %collective-permute-start.13 = (bf16[128,1536]{1,0:T(8,128)(2,1)S(1)}, bf16[128,1536]{1,0:T(8,128)(2,1)S(1)}, u32[]{:S(2)}, u32[]{:S(2)}) collective-permute-start(bf16[128,1536]{1,0:T(8,128)(2,1)S(1)} %pad_maximum_fusion.2), channel_id=1, source_target_pairs={{0,64},{64,128},{128,192},{192,0},{1,65},{65,129},{129,193},{193,1... | collective-permute-start | bytes 1179656 | tf_op jit(solution)/shard_map/ppermute | solution.py:19
  191.3 17.4 %collective-permute-start.14 = (bf16[128,1536]{1,0:T(8,128)(2,1)S(1)}, bf16[128,1536]{1,0:T(8,128)(2,1)S(1)}, u32[]{:S(2)}, u32[]{:S(2)}) collective-permute-start(bf16[128,1536]{1,0:T(8,128)(2,1)S(1)} %pad_maximum_fusion.3), channel_id=1, source_target_pairs={{0,192},{64,0},{128,64},{192,128},{1,193},{65,1},{129,65},{193,129... | collective-permute-start | bytes 1179656 | tf_op jit(solution)/shard_map/ppermute | solution.py:19
  197.9 24.4 %collective-permute-start.43 = (bf16[128,1536]{1,0:T(8,128)(2,1)S(1)}, bf16[128,1536]{1,0:T(8,128)(2,1)S(1)}, u32[]{:S(2)}, u32[]{:S(2)}) collective-permute-start(bf16[128,1536]{1,0:T(8,128)(2,1)S(1)} %get-tuple-element.31), channel_id=1, source_target_pairs={{0,128},{64,192},{128,0},{192,64},{1,129},{65,193},{129,1},{193,65... | collective-permute-start | bytes 1179656 | tf_op jit(solution)/shard_map/ppermute | solution.py:19
  208.6 16.3 %collective-permute-start.44 = (bf16[128,1536]{1,0:T(8,128)(2,1)S(1)}, bf16[128,1536]{1,0:T(8,128)(2,1)S(1)}, u32[]{:S(2)}, u32[]{:S(2)}) collective-permute-start(bf16[128,1536]{1,0:T(8,128)(2,1)S(1)} %get-tuple-element.31), channel_id=1, source_target_pairs={{0,192},{64,0},{128,64},{192,128},{1,193},{65,1},{129,65},{193,129... | collective-permute-start | bytes 1179656 | tf_op jit(solution)/shard_map/ppermute | solution.py:19
  222.0 20.9 %collective-permute-start.23 = (bf16[128,1536]{1,0:T(8,128)(2,1)S(1)}, bf16[128,1536]{1,0:T(8,128)(2,1)S(1)}, u32[]{:S(2)}, u32[]{:S(2)}) collective-permute-start(bf16[128,1536]{1,0:T(8,128)(2,1)S(1)} %get-tuple-element.24), channel_id=1, source_target_pairs={{0,128},{64,192},{128,0},{192,64},{1,129},{65,193},{129,1},{193,65... | collective-permute-start | bytes 1179656 | tf_op jit(solution)/shard_map/ppermute | solution.py:19
  222.3 20.5 %collective-permute-start.22 = (bf16[128,1536]{1,0:T(8,128)(2,1)S(1)}, bf16[128,1536]{1,0:T(8,128)(2,1)S(1)}, u32[]{:S(2)}, u32[]{:S(2)}) collective-permute-start(bf16[128,1536]{1,0:T(8,128)(2,1)S(1)} %get-tuple-element.24), channel_id=1, source_target_pairs={{0,64},{64,128},{128,192},{192,0},{1,65},{65,129},{129,193},{193,1... | collective-permute-start | bytes 1179656 | tf_op jit(solution)/shard_map/ppermute | solution.py:19
  225.0 18.0 %collective-permute-start.24 = (bf16[128,1536]{1,0:T(8,128)(2,1)S(1)}, bf16[128,1536]{1,0:T(8,128)(2,1)S(1)}, u32[]{:S(2)}, u32[]{:S(2)}) collective-permute-start(bf16[128,1536]{1,0:T(8,128)(2,1)S(1)} %get-tuple-element.24), channel_id=1, source_target_pairs={{0,192},{64,0},{128,64},{192,128},{1,193},{65,1},{129,65},{193,129... | collective-permute-start | bytes 1179656 | tf_op jit(solution)/shard_map/ppermute | solution.py:19
  229.7 20.7 %collective-permute-start.45 = (bf16[64,768]{1,0:T(8,128)(2,1)S(1)}, bf16[64,768]{1,0:T(8,128)(2,1)S(1)}, u32[]{:S(2)}, u32[]{:S(2)}) collective-permute-start(bf16[64,768]{1,0:T(8,128)(2,1)S(1)} %get-tuple-element.48), channel_id=1, source_target_pairs={{0,2},{2,4},{4,6},{6,8},{8,10},{10,12},{12,14},{14,0},{1,3},{3,5},... | collective-permute-start | bytes 294920 | tf_op jit(solution)/shard_map/ppermute | solution.py:19
  229.8 20.6 %collective-permute-start.49 = (bf16[64,768]{1,0:T(8,128)(2,1)S(1)}, bf16[64,768]{1,0:T(8,128)(2,1)S(1)}, u32[]{:S(2)}, u32[]{:S(2)}) collective-permute-start(bf16[64,768]{1,0:T(8,128)(2,1)S(1)} %get-tuple-element.50), channel_id=1, source_target_pairs={{0,14},{2,0},{4,2},{6,4},{8,6},{10,8},{12,10},{14,12},{1,15},{3,1}... | collective-permute-start | bytes 294920 | tf_op jit(solution)/shard_map/ppermute | solution.py:19
  253.7 19.2 %collective-permute-start.33 = (bf16[64,1536]{1,0:T(8,128)(2,1)S(1)}, bf16[64,1536]{1,0:T(8,128)(2,1)S(1)}, u32[]{:S(2)}, u32[]{:S(2)}) collective-permute-start(bf16[64,1536]{1,0:T(8,128)(2,1)S(1)} %pad_maximum_fusion.12), channel_id=1, source_target_pairs={{0,14},{2,0},{4,2},{6,4},{8,6},{10,8},{12,10},{14,12},{1,15},{3,1}... | collective-permute-start | bytes 589832 | tf_op jit(solution)/shard_map/ppermute | solution.py:19
  (44 other events, 366.3 us)
Sparse Core Ops, SparseCore 0:
  32.2 46.9 all-gather.4
  81.0 43.6 all-gather.6
